TPU v7x, 32 devices: a whole 2x2x4 slice. The times are simulated.
32 devices in a mesh: band: 8 (over z, core), dom: 4 (over y, x).
Axes of the slice: x: 2, y: 2, z: 4, core: 2. Of those that a mesh axis runs over, the one named last changes fastest.
Arguments:
- orbitals: bfloat16 [512, 24576], P('band', 'dom'), may hold values from -6 to 6
- rotation: bfloat16 [512, 256], P('band'), may hold values from -0.375 to 0.375
- projectors: bfloat16 [32, 16, 24576], P(None, None, 'dom'), may hold values from -0.078125 to 0.078125
- coupling: float32 [64, 16, 16], P('dom'), may hold values from -5 to 5
- slot_atom: int32 [4, 32], replicated, may hold values from 0 to 63, as said below
Outputs:
- updated_orbitals: bfloat16 [512, 24576], P('band', 'dom')
Inputs may be any that keep to these rules, and one draw needn't show every extreme that they name: `slot_atom`: the atoms of one row are distinct. Atom a is owned by domain a // 16. A row names at most 16 atoms of any one owner; domain 4 - 1 is named exactly 16 times by every row. Other owners are named between 0 and 16 times, unevenly.
All inputs are finite; a program needn't handle non-finite values.
Results may differ from a plain program's by a relative error of at most 0.0057.
Values may be sent and summed in bfloat16 or wider, within the bound.
No kernel may reach another device: no remote copies, remote signals or barrier semaphores. Data moves between devices by JAX's collectives and lax.ppermute only.
A program may use at most 64 MiB of HBM per device.

v0:
```python
import jax
import jax.numpy as jnp
from jax import lax
from jax.sharding import PartitionSpec as P


def passed_along(block, axis, distance):
    devices = range(lax.axis_size(axis))
    route = [((i - distance) % len(devices), i) for i in devices]
    return lax.ppermute(block, axis, route)


def couple_atoms(coupling, summed, proj_count):
    atom_count = summed.shape[0]
    shaped = summed.reshape(atom_count, proj_count, -1)
    coupled = jnp.einsum("apq,aqo->apo", coupling, shaped, precision=lax.Precision.HIGHEST)
    return coupled.astype(jnp.bfloat16).reshape(atom_count, -1)


def on_device(orbitals, rotation, projectors, coupling, slot_atom):
    width = orbitals.shape[0]
    stop_count = rotation.shape[1] // width
    running = jnp.dot(rotation[:, :width], orbitals, preferred_element_type=jnp.float32)
    moving = orbitals
    for stop_index in range(1, stop_count):
        moving = passed_along(moving, "band", 1)
        running = running + jnp.dot(
            rotation[:, stop_index * width : (stop_index + 1) * width],
            moving,
            preferred_element_type=jnp.float32,
        )
    rotated = running.astype(jnp.bfloat16)
    slot_count = projectors.shape[0]
    proj_count = projectors.shape[1]
    partial_value = jnp.einsum(
        "kpg,og->kpo", projectors, rotated, preferred_element_type=jnp.float32
    ).reshape(slot_count, -1)
    domain_index = lax.axis_index("dom")
    domain_count = lax.axis_size("dom")
    owned = coupling.shape[0]
    own_atoms = lax.dynamic_index_in_dim(slot_atom, domain_index, 0, keepdims=False)
    capacity = max(min(4, owned), (2 * slot_count + domain_count - 1) // domain_count)
    owners_all = slot_atom // owned
    positions = jnp.arange(slot_count, dtype=jnp.int32)
    earlier = (owners_all[:, :, None] == owners_all[:, None, :]) & (
        positions[None, None, :] < positions[None, :, None]
    )
    ranks_all = jnp.sum(earlier.astype(jnp.int32), axis=2)
    own_owner = own_atoms // owned
    own_rank = lax.dynamic_index_in_dim(ranks_all, domain_index, 0, keepdims=False)
    slot_place = own_owner * capacity + own_rank
    buffer_rows = jnp.arange(domain_count * capacity, dtype=jnp.int32)
    placing = (buffer_rows[:, None] == slot_place[None, :]).astype(jnp.float32)
    outgoing = jnp.dot(placing, partial_value, precision=lax.Precision.HIGHEST).reshape(
        domain_count, capacity, -1
    )
    incoming = lax.all_to_all(outgoing, "dom", split_axis=0, concat_axis=0, tiled=True)
    mine = (owners_all == domain_index)[:, :, None, None]
    rank_match = (
        ranks_all[:, :, None, None] == jnp.arange(capacity, dtype=jnp.int32)[None, None, :, None]
    )
    atom_match = (slot_atom % owned)[:, :, None, None] == jnp.arange(owned, dtype=jnp.int32)[
        None, None, None, :
    ]
    selector = jnp.sum((mine & rank_match & atom_match).astype(jnp.float32), axis=1)
    summed = jnp.einsum("jca,jcx->ax", selector, incoming, precision=lax.Precision.HIGHEST)
    coupled = couple_atoms(coupling, summed, proj_count)
    answers = jnp.einsum(
        "jca,ax->jcx", selector, coupled.astype(jnp.float32), precision=lax.Precision.HIGHEST
    ).astype(jnp.bfloat16)
    replies = lax.all_to_all(answers, "dom", split_axis=0, concat_axis=0, tiled=True)
    returned = jnp.take(replies.reshape(domain_count * capacity, -1), slot_place, axis=0)
    applied = jnp.einsum(
        "kpg,kpo->og",
        projectors,
        returned.reshape(slot_count, proj_count, width),
        preferred_element_type=jnp.float32,
    )
    return (rotated.astype(jnp.float32) + applied).astype(jnp.bfloat16)


def solution(mesh):
    in_specs = (P("band", "dom"), P("band", None), P(None, None, "dom"), P("dom", None, None), P())
    out_specs = P("band", "dom")
    return jax.shard_map(
        on_device, mesh=mesh, in_specs=in_specs, out_specs=out_specs, check_vma=False
    )
```

profile of v0, /device:TPU:0, one launch (start us, length us, event | category | flops | bytes accessed | tf_op | source)
XLA Modules:
  0.0 74.9 jit_solution(7923375030844528299)
XLA Ops:
  0.0 0.0 copy-start
  0.0 0.0 copy-start.3
  0.0 0.0 copy-start.2
  0.0 0.5 collective-permute-start
  0.5 0.7 broadcast_compare_fusion
  1.2 0.2 convert_reduce_fusion.1
  1.4 13.0 %collective-permute-done = bf16[64,6144]{1,0:T(8,128)(2,1)S(1)} collective-permute-done((bf16[64,6144]{1,0:T(8,128)(2,1)}, bf16[64,6144]{1,0:T(8,128)(2,1)S(1)}, u32[]{:S(2)}, u32[]{:S(2)}) %collective-permute-start) | collective-permute-done | bytes 786464 | tf_op jit(solution)/shard_map/ppermute | solution.py:10
  14.4 0.0 collective-permute-start.1
  14.4 0.7 add_bitcast_fusion
  15.1 0.7 add_select_fusion
  15.9 1.5 %fusion.24 = f32[64,6144]{1,0:T(8,128)S(1)} fusion(bf16[64,6144]{1,0:T(8,128)(2,1)} %param.5, bf16[64,256]{1,0:T(8,128)(2,1)} %param.6), kind=kOutput, calls=%fused_computation.35 | convolution fusion | flops 50331648 | bytes 2375680 | tf_op jit(solution)/shard_map/dot_general | solution.py:23
  17.4 10.3 %collective-permute-done.1 = bf16[64,6144]{1,0:T(8,128)(2,1)S(1)} collective-permute-done((bf16[64,6144]{1,0:T(8,128)(2,1)S(1)}, bf16[64,6144]{1,0:T(8,128)(2,1)S(1)}, u32[]{:S(2)}, u32[]{:S(2)}) %collective-permute-start.1) | collective-permute-done | bytes 786464 | tf_op jit(solution)/shard_map/ppermute | solution.py:10
  27.7 0.0 collective-permute-start.2
  27.7 0.0 copy-done.3
  27.7 0.0 copy-done.2
  27.7 0.4 convolution_add_fusion.2
  28.1 0.0 copy-start.1
  28.1 0.3 convolution_add_fusion.1
  28.5 12.4 %collective-permute-done.2 = bf16[64,6144]{1,0:T(8,128)(2,1)S(1)} collective-permute-done((bf16[64,6144]{1,0:T(8,128)(2,1)S(1)}, bf16[64,6144]{1,0:T(8,128)(2,1)S(1)}, u32[]{:S(2)}, u32[]{:S(2)}) %collective-permute-start.2) | collective-permute-done | bytes 786464 | tf_op jit(solution)/shard_map/ppermute | solution.py:10
  40.9 0.4 fusion
  41.3 0.0 copy-done.1
  41.3 4.2 %fusion.4 = f32[32,16,64]{2,0,1:T(8,128)S(1)} fusion(bf16[32,16,6144]{2,1,0:T(8,128)(2,1)S(1)} %copy-done.1, bf16[64,6144]{1,0:T(8,128)(2,1)S(1)} %fusion), kind=kOutput, calls=%fused_computation.10 | convolution fusion | flops 402653184 | bytes 7208960 | tf_op jit(solution)/shard_map/kpg,og->kpo/dot_general | solution.py:35
  45.5 0.2 copy.14
  45.6 0.1 reshape.186
  45.8 1.0 %fusion.17 = f32[4,16,1024]{2,1,0:T(8,128)} fusion(f32[32,1024,1]{1,0,2:T(8,128)S(1)} %reshape.186, s32[32]{0:T(128)S(1)} %add_bitcast_fusion, s32[4,16]{1,0:T(4,128)S(1)} %multiply_add_fusion), kind=kOutput, calls=%fused_computation.27 | convolution fusion | flops 25167872 | bytes 393600 | tf_op jit(solution)/shard_map/dot_general | solution.py:54
  46.8 4.2 %all-to-all-start = ((f32[4,16,1024]{2,1,0:T(8,128)}), f32[4,16,1024]{2,1,0:T(8,128)S(1)}, u32[]{:S(2)}, u32[]{:S(2)}) async-start(f32[4,16,1024]{2,1,0:T(8,128)} %fusion.17), calls=%async_computation | async-start | bytes 524288 | tf_op jit(solution)/shard_map/all_to_all | solution.py:57
  51.0 0.2 convert_reduce_fusion
  51.2 5.1 %all-to-all-done = f32[4,16,1024]{2,1,0:T(8,128)S(1)} async-done(((f32[4,16,1024]{2,1,0:T(8,128)}), f32[4,16,1024]{2,1,0:T(8,128)S(1)}, u32[]{:S(2)}, u32[]{:S(2)}) %all-to-all-start) | async-done | bytes 262176 | tf_op jit(solution)/shard_map/all_to_all | solution.py:57
  56.4 0.1 dot_general.44
  56.5 0.5 convolution_bitcast_fusion.1
  57.0 0.0 copy-done
  57.0 0.3 fusion.7
  57.3 0.1 reshape.189
  57.4 0.9 %convolution_convert_fusion = bf16[4,16,1024]{2,1,0:T(8,128)(2,1)} fusion(f32[4,16,16]{2,1,0:T(8,128)S(1)} %convert_reduce_fusion, bf16[16,1024,1]{1,0,2:T(8,128)(2,1)S(1)} %reshape.189), kind=kOutput, calls=%fused_computation.11 | convolution fusion | flops 12648448 | bytes 167936 | tf_op jit(solution)/shard_map/jca,ax->jcx/dot_general | solution.py:68
  58.3 3.3 %all-to-all-start.1 = ((bf16[4,16,1024]{2,1,0:T(8,128)(2,1)}), bf16[4,16,1024]{2,1,0:T(8,128)(2,1)S(1)}, u32[]{:S(2)}, u32[]{:S(2)}) async-start(bf16[4,16,1024]{2,1,0:T(8,128)(2,1)} %convolution_convert_fusion), calls=%async_computation.1 | async-start | bytes 262144 | tf_op jit(solution)/shard_map/all_to_all | solution.py:71
  61.7 5.0 %all-to-all-done.1 = bf16[4,16,1024]{2,1,0:T(8,128)(2,1)S(1)} async-done(((bf16[4,16,1024]{2,1,0:T(8,128)(2,1)}), bf16[4,16,1024]{2,1,0:T(8,128)(2,1)S(1)}, u32[]{:S(2)}, u32[]{:S(2)}) %all-to-all-start.1) | async-done | bytes 131104 | tf_op jit(solution)/shard_map/all_to_all | solution.py:71
  66.7 0.6 gather_fusion
  67.3 0.1 gather.7
  67.4 7.4 %add_convert_fusion = bf16[64,6144]{1,0:T(8,128)(2,1)} fusion(bf16[64,6144]{1,0:T(8,128)(2,1)S(1)} %fusion, bf16[32,16,6144]{2,1,0:T(8,128)(2,1)} %param.7, bf16[32,16,64]{2,1,0:T(8,128)(2,1)S(1)} %gather.7, pred[32]{0:T(512)(128)(4,1)S(1)} %compare_and_fusion), kind=kOutput, calls=%fused_computation.9 | convolution fusion | flops 403865600 | bytes 7929888 | tf_op jit(solution)/shard_map/kpg,kpo->og/dot_general | solution.py:73
  (6 shorter events, 0.1 us)
Async XLA Ops:
  0.0 57.0 %copy-start = (f32[16,16,16]{2,1,0:T(8,128)S(1)}, f32[16,16,16]{2,1,0:T(8,128)}, u32[]{:S(2)}) copy-start(f32[16,16,16]{2,1,0:T(8,128)} %param.8) | copy-start | bytes 49156
  0.0 27.7 %copy-start.3 = (s32[4,32]{1,0:T(4,128)S(1)}, s32[4,32]{1,0:T(4,128)}, u32[]{:S(2)}) copy-start(s32[4,32]{1,0:T(4,128)} %param.9) | copy-start | bytes 1540
  0.0 27.7 %copy-start.2 = (bf16[64,256]{1,0:T(8,128)(2,1)S(1)}, bf16[64,256]{1,0:T(8,128)(2,1)}, u32[]{:S(2)}) copy-start(bf16[64,256]{1,0:T(8,128)(2,1)} %param.6) | copy-start | bytes 98308
  0.0 14.4 %collective-permute-start = (bf16[64,6144]{1,0:T(8,128)(2,1)}, bf16[64,6144]{1,0:T(8,128)(2,1)S(1)}, u32[]{:S(2)}, u32[]{:S(2)}) collective-permute-start(bf16[64,6144]{1,0:T(8,128)(2,1)} %param.5), channel_id=1, source_target_pairs={{28,0},{0,4},{4,8},{8,12},{12,16},{16,20},{20,24},{24,28},{29,1},{... | collective-permute-start | bytes 2359304 | tf_op jit(solution)/shard_map/ppermute | solution.py:10
  14.4 13.2 %collective-permute-start.1 = (bf16[64,6144]{1,0:T(8,128)(2,1)S(1)}, bf16[64,6144]{1,0:T(8,128)(2,1)S(1)}, u32[]{:S(2)}, u32[]{:S(2)}) collective-permute-start(bf16[64,6144]{1,0:T(8,128)(2,1)S(1)} %collective-permute-done), channel_id=1, source_target_pairs={{28,0},{0,4},{4,8},{8,12},{12,16},{16,20},{20,24},{24,28},{29,1},{... | collective-permute-start | bytes 2359304 | tf_op jit(solution)/shard_map/ppermute | solution.py:10
  27.7 13.2 %collective-permute-start.2 = (bf16[64,6144]{1,0:T(8,128)(2,1)S(1)}, bf16[64,6144]{1,0:T(8,128)(2,1)S(1)}, u32[]{:S(2)}, u32[]{:S(2)}) collective-permute-start(bf16[64,6144]{1,0:T(8,128)(2,1)S(1)} %collective-permute-done.1), channel_id=1, source_target_pairs={{28,0},{0,4},{4,8},{8,12},{12,16},{16,20},{20,24},{24,28},{29,1},{... | collective-permute-start | bytes 2359304 | tf_op jit(solution)/shard_map/ppermute | solution.py:10
  28.1 13.2 %copy-start.1 = (bf16[32,16,6144]{2,1,0:T(8,128)(2,1)S(1)}, bf16[32,16,6144]{2,1,0:T(8,128)(2,1)}, u32[]{:S(2)}) copy-start(bf16[32,16,6144]{2,1,0:T(8,128)(2,1)} %param.7) | copy-start | bytes 18874372
  46.8 9.6 %all-to-all-start = ((f32[4,16,1024]{2,1,0:T(8,128)}), f32[4,16,1024]{2,1,0:T(8,128)S(1)}, u32[]{:S(2)}, u32[]{:S(2)}) async-start(f32[4,16,1024]{2,1,0:T(8,128)} %fusion.17), calls=%async_computation | async-start | bytes 524288 | tf_op jit(solution)/shard_map/all_to_all | solution.py:57
  58.3 8.3 %all-to-all-start.1 = ((bf16[4,16,1024]{2,1,0:T(8,128)(2,1)}), bf16[4,16,1024]{2,1,0:T(8,128)(2,1)S(1)}, u32[]{:S(2)}, u32[]{:S(2)}) async-start(bf16[4,16,1024]{2,1,0:T(8,128)(2,1)} %convolution_convert_fusion), calls=%async_computation.1 | async-start | bytes 262144 | tf_op jit(solution)/shard_map/all_to_all | solution.py:71
where the time goes:
time: 75.3 us; the launch traced here: 74.9 us
  waiting for transfers between devices  45.8 us (61%)
  matrix products  17 us (23%)
  starting transfers between devices  8.05 us (11%)
  other arithmetic  2.58 us (3%)
  local copies, waits for them, and re-layouts  1.32 us (2%)
    ppermute x3, waiting for transfers between devices, passed_along(): return lax.ppermute(block, axis, route)  35.7 us
    dot_general x1, matrix products, on_device(): jnp.einsum('kpg,kpo->og', projectors, returned.reshape(slot_count, proj_c...  7.43 us
    all_to_all x1, waiting for transfers between devices, on_device(): lax.all_to_all(outgoing, 'dom', split_axis=0, concat_axis=0, tiled=True)  5.14 us
    all_to_all x1, waiting for transfers between devices, on_device(): lax.all_to_all(answers, 'dom', split_axis=0, concat_axis=0, tiled=True)  4.96 us
    all_to_all x1, starting transfers between devices, on_device(): lax.all_to_all(outgoing, 'dom', split_axis=0, concat_axis=0, tiled=True)  4.21 us
    dot_general x1, matrix products, on_device(): jnp.einsum('kpg,og->kpo', projectors, rotated, preferred_element_type=jnp...  4.18 us
    all_to_all x1, starting transfers between devices, on_device(): lax.all_to_all(answers, 'dom', split_axis=0, concat_axis=0, tiled=True)  3.33 us
  transfers between devices with their start and end apart: 5, of which 5 were waited for; matrix products, arithmetic and copies ran while one was open for 6% of the time, Pallas kernels for 0%

commit v1 on v0

v1 whole, which is shorter than its diff:
```python
import jax
import jax.numpy as jnp
from jax import lax
from jax.sharding import PartitionSpec as P

PARTS = 4


def passed_along(block, axis, distance):
    devices = range(lax.axis_size(axis))
    route = [((i - distance) % len(devices), i) for i in devices]
    return lax.ppermute(block, axis, route)


def from_all_domains(block):
    count = lax.axis_size("dom")
    me = lax.axis_index("dom")
    if count <= 8 and count & (count - 1) == 0:
        pairs = [(me, block)]
        for mask in range(1, count):
            route = [(i, i ^ mask) for i in range(count)]
            pairs.append((me ^ mask, lax.ppermute(block, "dom", route)))
        return pairs
    whole = lax.all_gather(block, "dom")
    return [(jnp.int32(d), whole[d]) for d in range(count)]


def on_device(orbitals, rotation, projectors, coupling, slot_atom):
    width, points = orbitals.shape
    stop_count = rotation.shape[1] // width
    slot_count, proj_count, _ = projectors.shape
    flat = slot_count * proj_count
    proj = projectors.reshape(flat, points)
    tiles = [rotation[:, s * width : (s + 1) * width] for s in range(stop_count)]
    step = points // PARTS

    coef = lax.dot_general(
        orbitals, proj, (((1,), (1,)), ((), ())), preferred_element_type=jnp.float32
    ).astype(jnp.bfloat16)

    held = [[orbitals[:, j * step : (j + 1) * step]] for j in range(PARTS)]
    held_coef = [coef]
    for s in range(1, stop_count):
        for j in range(PARTS):
            held[j].append(passed_along(held[j][-1], "band", 1))
        held_coef.append(passed_along(held_coef[-1], "band", 1))

    def rotate(blocks):
        return sum(
            jnp.dot(t, x, preferred_element_type=jnp.float32) for t, x in zip(tiles, blocks)
        )

    me = lax.axis_index("dom")
    own_atoms = lax.dynamic_index_in_dim(slot_atom, me, 0, keepdims=False)
    coupling_all = lax.all_gather(coupling, "dom", tiled=True)
    mine = jnp.take(coupling_all, own_atoms, axis=0)
    columns = mine.transpose(2, 0, 1).reshape(proj_count, flat)
    own_wide = jnp.repeat(own_atoms, proj_count)[None, :]
    tall = jnp.broadcast_to(columns[None], (slot_count, proj_count, flat)).reshape(flat, flat)

    rotated_coef = rotate(held_coef)
    coupled = None
    for d, block in from_all_domains(rotated_coef):
        theirs = lax.dynamic_index_in_dim(slot_atom, d, 0, keepdims=False)
        weights = jnp.where(jnp.repeat(theirs, proj_count)[:, None] == own_wide, tall, 0.0)
        term = jnp.dot(block, weights, precision=lax.Precision.HIGHEST)
        coupled = term if coupled is None else coupled + term
    coupled = coupled.astype(jnp.bfloat16)

    outs = []
    for j in range(PARTS):
        applied = jnp.dot(
            coupled, proj[:, j * step : (j + 1) * step], preferred_element_type=jnp.float32
        )
        rotated = rotate(held[j]).astype(jnp.bfloat16).astype(jnp.float32)
        outs.append((rotated + applied).astype(jnp.bfloat16))
    return jnp.concatenate(outs, axis=1)


def solution(mesh):
    in_specs = (P("band", "dom"), P("band", None), P(None, None, "dom"), P("dom", None, None), P())
    out_specs = P("band", "dom")
    return jax.shard_map(
        on_device, mesh=mesh, in_specs=in_specs, out_specs=out_specs, check_vma=False
    )
```

time: 75.3 us -> 66 us (0.88)
  waiting for transfers between devices: 45.8 us -> 23.6 us
  blocking collectives: 0 us -> 11.4 us
  matrix products: 17 us -> 18.5 us
  other arithmetic: 2.58 us -> 1.42 us
  starting transfers between devices: 8.05 us -> 9.1 us
    ppermute x3 -> x15, waiting for transfers between devices: 35.7 us -> 23.6 us  [passed_along(): return lax.ppermute(block, axis, route)]
    all_gather x0 -> x1, blocking collectives: none -> 11.4 us  [on_device(): coupling_all = lax.all_gather(coupling, 'dom', tiled=True)]
    all_to_all x2 -> x0, waiting for transfers between devices: 10.1 us -> none  [the longest x1 5.14 us: on_device(): lax.all_to_all(outgoing, 'dom', split_axis=0, concat_axis=0, tiled=True)]
    all_to_all x2 -> x0, starting transfers between devices: 7.53 us -> none  [the longest x1 4.21 us: on_device(): lax.all_to_all(outgoing, 'dom', split_axis=0, concat_axis=0, tiled=True)]
    ppermute x3 -> x15, starting transfers between devices: 0.52 us -> 5.41 us  [passed_along(): return lax.ppermute(block, axis, route)]
    ppermute x0 -> x3, starting transfers between devices: none -> 3.68 us  [from_all_domains(): pairs.append((me ^ mask, lax.ppermute(block, 'dom', route)))]
    dot_general x10 -> x29, matrix products: 17 us -> 18.5 us  [the longest x20 8.76 us: rotate(): jnp.dot(t, x, preferred_element_type=jnp.float32)]
    eq x4 -> x0, other arithmetic: 1.41 us -> none  [the longest x2 0.7 us: on_device(): placing = (buffer_rows[:, None] == slot_place[None, :]).astype(jnp.float32)]
  transfers between devices with their start and end apart: 5 -> 18, of which waited for: 5 -> 10; matrix products, arithmetic and copies ran while one was open for 6% -> 23% of each run, Pallas kernels for 0% -> 0%
where the time goes in v1:
time: 66 us; the launch traced here: 65.8 us
  waiting for transfers between devices  23.6 us (36%)
  matrix products  18.5 us (28%)
  blocking collectives  11.4 us (17%)
  starting transfers between devices  9.1 us (14%)
  other arithmetic  1.42 us (2%)
  local copies, waits for them, and re-layouts  1.4 us (2%)
    ppermute x15, waiting for transfers between devices, passed_along(): return lax.ppermute(block, axis, route)  23.6 us
    all_gather x1, blocking collectives, on_device(): coupling_all = lax.all_gather(coupling, 'dom', tiled=True)  11.4 us
    dot_general x20, matrix products, rotate(): jnp.dot(t, x, preferred_element_type=jnp.float32)  8.76 us
    ppermute x15, starting transfers between devices, passed_along(): return lax.ppermute(block, axis, route)  5.41 us
    dot_general x1, matrix products, on_device(): lax.dot_general(orbitals, proj, (((1,), (1,)), ((), ())), preferred_eleme...  5.12 us
    ppermute x3, starting transfers between devices, from_all_domains(): pairs.append((me ^ mask, lax.ppermute(block, 'dom', route)))  3.68 us
    dot_general x4, matrix products, on_device(): term = jnp.dot(block, weights, precision=lax.Precision.HIGHEST)  3.02 us
    dot_general x4, matrix products, on_device(): jnp.dot(coupled, proj[:, j * step:(j + 1) * step], preferred_element_type...  1.56 us
  transfers between devices with their start and end apart: 18, of which 10 were waited for; matrix products, arithmetic and copies ran while one was open for 23% of the time, Pallas kernels for 0%

profile of v1, /device:TPU:0, one launch (start us, length us, event | category | flops | bytes accessed | tf_op | source)
XLA Modules:
  0.0 65.8 jit_solution(5800937545580798809)
XLA Ops:
  0.0 5.1 %convolution_convert_fusion = bf16[64,512]{1,0:T(8,128)(2,1)S(1)} fusion(bf16[64,6144]{1,0:T(8,128)(2,1)} %param.5, bf16[512,6144]{1,0:T(8,128)(2,1)} %bitcast.53), kind=kOutput, calls=%fused_computation.48 | convolution fusion | flops 402685952 | bytes 7143424 | tf_op jit(solution)/shard_map/dot_general | solution.py:37
  5.2 0.5 collective-permute-start.3
  5.7 2.7 %collective-permute-start.12 = (bf16[64,1536]{1,0:T(8,128)(2,1)S(1)}, bf16[64,1536]{1,0:T(8,128)(2,1)}, u32[]{:S(2)}, u32[]{:S(2)}) collective-permute-start(bf16[64,1536]{1,0:T(8,128)(2,1)S(1)} %get-tuple-element.10), channel_id=1, source_target_pairs={{28,0},{0,4},{4,8},{8,12},{12,16},{16,20},{20,24},{24,28},{29,1},{... | collective-permute-start | bytes 589832 | tf_op jit(solution)/shard_map/ppermute | solution.py:12
  8.5 0.1 collective-permute-start
  8.5 1.6 %collective-permute-start.9 = (bf16[64,1536]{1,0:T(8,128)(2,1)S(1)}, bf16[64,1536]{1,0:T(8,128)(2,1)}, u32[]{:S(2)}, u32[]{:S(2)}) collective-permute-start(bf16[64,1536]{1,0:T(8,128)(2,1)S(1)} %get-tuple-element.8), channel_id=1, source_target_pairs={{28,0},{0,4},{4,8},{8,12},{12,16},{16,20},{20,24},{24,28},{29,1},{... | collective-permute-start | bytes 589832 | tf_op jit(solution)/shard_map/ppermute | solution.py:12
  10.2 0.1 collective-permute-start.15
  10.3 0.1 fusion.47
  10.4 0.2 fusion.43
  10.6 0.2 fusion.49
  10.8 0.2 fusion.45
  11.0 0.2 fusion.41
  11.2 11.4 %all_gather.3 = f32[64,16,16]{2,1,0:T(8,128)S(1)} all-gather(f32[16,16,16]{2,1,0:T(8,128)S(1)} %copy-done.2), channel_id=1, replica_groups=mesh['band'=8,'dom'=4] {'dom'}, dimensions={0}, use_global_device_ids=true | all-gather | bytes 81920 | tf_op jit(solution)/shard_map/all_gather | solution.py:55
  22.6 0.6 gather_fusion
  23.2 0.1 broadcast_select_fusion
  23.3 0.1 broadcast_in_dim.43
  23.4 0.1 eq.58
  23.5 0.1 broadcast_in_dim.44
  23.6 0.1 eq.61
  23.6 0.1 broadcast_in_dim.45
  23.7 0.1 eq.64
  23.8 0.1 copy.8
  23.9 0.1 broadcast_in_dim.37
  24.0 0.1 eq.26
  24.1 0.4 bitcast_select_fusion.1
  24.4 0.2 collective-permute-start.4
  24.6 1.1 %convolution_add_fusion.16 = f32[512,64]{0,1:T(8,128)S(1)} fusion(f32[512,64]{0,1:T(8,128)S(1)} %fusion.47, bf16[64,512]{1,0:T(8,128)(2,1)} %collective-permute-done.3, bf16[64,256]{1,0:T(8,128)(2,1)S(1)} %copy-done.1), kind=kOutput, calls=%fused_computation.46 | convolution fusion | flops 4227072 | bytes 344064 | tf_op jit(solution)/shard_map/dot_general | solution.py:50
  25.7 4.4 %collective-permute-done.4 = bf16[64,512]{1,0:T(8,128)(2,1)S(1)} collective-permute-done((bf16[64,512]{1,0:T(8,128)(2,1)}, bf16[64,512]{1,0:T(8,128)(2,1)S(1)}, u32[]{:S(2)}, u32[]{:S(2)}) %collective-permute-start.4) | collective-permute-done | bytes 65568 | tf_op jit(solution)/shard_map/ppermute | solution.py:12
  30.2 0.1 convolution_add_fusion.15
  30.3 5.3 %collective-permute-done.5 = bf16[64,512]{1,0:T(8,128)(2,1)S(1)} collective-permute-done((bf16[64,512]{1,0:T(8,128)(2,1)S(1)}, bf16[64,512]{1,0:T(8,128)(2,1)S(1)}, u32[]{:S(2)}, u32[]{:S(2)}) %collective-permute-start.5) | collective-permute-done | bytes 65568 | tf_op jit(solution)/shard_map/ppermute | solution.py:12
  35.7 0.2 convolution_add_fusion.14
  35.9 1.6 %collective-permute-start.6 = (f32[64,512]{1,0:T(8,128)S(1)}, f32[64,512]{1,0:T(8,128)S(1)}, u32[]{:S(2)}, u32[]{:S(2)}) collective-permute-start(f32[64,512]{1,0:T(8,128)S(1)} %bitcast.61), channel_id=1, source_target_pairs={{0,1},{1,0},{2,3},{3,2},{4,5},{5,4},{6,7},{7,6},{8,9},{9,8},{10,11... | collective-permute-start | bytes 393224 | tf_op jit(solution)/shard_map/ppermute | solution.py:22
  37.4 0.8 %fusion.62 = f32[64,512]{1,0:T(8,128)S(1)} fusion(f32[512,64]{0,1:T(8,128)S(1)} %convolution_add_fusion.14, f32[512,512]{1,0:T(8,128)S(1)} %get-tuple-element.14), kind=kOutput, calls=%fused_computation.94 | convolution fusion | flops 201326592 | bytes 1310720 | tf_op jit(solution)/shard_map/dot_general | solution.py:66
  38.2 1.5 %collective-permute-start.8 = (f32[64,512]{1,0:T(8,128)S(1)}, f32[64,512]{1,0:T(8,128)S(1)}, u32[]{:S(2)}, u32[]{:S(2)}) collective-permute-start(f32[64,512]{1,0:T(8,128)S(1)} %bitcast.62), channel_id=1, source_target_pairs={{0,3},{1,2},{2,1},{3,0},{4,7},{5,6},{6,5},{7,4},{8,11},{9,10},{10,... | collective-permute-start | bytes 393224 | tf_op jit(solution)/shard_map/ppermute | solution.py:22
  39.7 1.2 %convolution_add_fusion.5 = f32[64,1536]{1,0:T(8,128)S(1)} fusion(f32[64,1536]{1,0:T(8,128)S(1)} %fusion.43, bf16[64,1536]{1,0:T(8,128)(2,1)} %collective-permute-done.12, bf16[64,256]{1,0:T(8,128)(2,1)S(1)} %copy-done.1), kind=kOutput, calls=%fused_computation.10 | convolution fusion | flops 12681216 | bytes 999424 | tf_op jit(solution)/shard_map/dot_general | solution.py:50
  40.9 0.6 collective-permute-start.7
  41.5 1.2 %convolution_add_fusion.11 = f32[64,1536]{1,0:T(8,128)S(1)} fusion(f32[64,1536]{1,0:T(8,128)S(1)} %fusion.49, bf16[64,1536]{1,0:T(8,128)(2,1)} %collective-permute-done, bf16[64,256]{1,0:T(8,128)(2,1)S(1)} %copy-done.1), kind=kOutput, calls=%fused_computation.16 | convolution fusion | flops 12681216 | bytes 999424 | tf_op jit(solution)/shard_map/dot_general | solution.py:50
  42.7 0.1 collective-permute-start.13
  42.8 1.2 %convolution_add_fusion.8 = f32[64,1536]{1,0:T(8,128)S(1)} fusion(f32[64,1536]{1,0:T(8,128)S(1)} %fusion.45, bf16[64,1536]{1,0:T(8,128)(2,1)} %collective-permute-done.9, bf16[64,256]{1,0:T(8,128)(2,1)S(1)} %copy-done.1), kind=kOutput, calls=%fused_computation.13 | convolution fusion | flops 12681216 | bytes 999424 | tf_op jit(solution)/shard_map/dot_general | solution.py:50
  44.0 0.1 collective-permute-start.1
  44.0 1.2 %convolution_add_fusion.2 = f32[64,1536]{1,0:T(8,128)S(1)} fusion(f32[64,1536]{1,0:T(8,128)S(1)} %fusion.41, bf16[64,1536]{1,0:T(8,128)(2,1)} %collective-permute-done.15, bf16[64,256]{1,0:T(8,128)(2,1)S(1)} %copy-done.1), kind=kOutput, calls=%fused_computation.7 | convolution fusion | flops 12681216 | bytes 999424 | tf_op jit(solution)/shard_map/dot_general | solution.py:50
  45.3 0.8 %convolution_add_fusion.13 = f32[64,512]{1,0:T(8,128)S(1)} fusion(f32[64,512]{1,0:T(8,128)S(1)} %fusion.62, f32[64,512]{1,0:T(8,128)S(1)} %collective-permute-done.6, f32[512,512]{1,0:T(8,128)S(1)} %get-tuple-element.13), kind=kOutput, calls=%fused_computation.42 | convolution fusion | flops 201359360 | bytes 1441792 | tf_op jit(solution)/shard_map/dot_general | solution.py:66
  46.1 0.8 %fusion.63 = f32[64,512]{1,0:T(8,128)S(1)} fusion(f32[64,512]{1,0:T(8,128)S(1)} %collective-permute-done.8, f32[512,512]{1,0:T(8,128)S(1)} %get-tuple-element.12), kind=kOutput, calls=%fused_computation.95 | convolution fusion | flops 201326592 | bytes 1310720 | tf_op jit(solution)/shard_map/dot_general | solution.py:66
  46.9 0.8 %fusion.25 = bf16[64,512]{1,0:T(8,128)(2,1)S(1)} fusion(f32[64,512]{1,0:T(8,128)S(1)} %fusion.63, f32[64,512]{1,0:T(8,128)S(1)} %convolution_add_fusion.13, f32[64,512]{1,0:T(8,128)S(1)} %collective-permute-done.7, f32[512,512]{1,0:T(8,128)S(1)} %get-tuple-element.11), kind=kOutput, calls=%fused_computation.47 | convolution fusion | flops 201424896 | bytes 1507328 | tf_op jit(solution)/shard_map/dot_general | solution.py:66
  47.7 0.4 fusion.18
  48.1 0.4 fusion.22
  48.4 0.4 fusion.20
  48.8 0.4 fusion.16
  49.2 0.6 collective-permute-done.13
  49.9 0.2 convolution_add_fusion.4
  50.1 1.9 %collective-permute-done.1 = bf16[64,1536]{1,0:T(8,128)(2,1)S(1)} collective-permute-done((bf16[64,1536]{1,0:T(8,128)(2,1)}, bf16[64,1536]{1,0:T(8,128)(2,1)S(1)}, u32[]{:S(2)}, u32[]{:S(2)}) %collective-permute-start.1) | collective-permute-done | bytes 196640 | tf_op jit(solution)/shard_map/ppermute | solution.py:12
  52.0 0.2 convolution_add_fusion.10
  52.2 1.9 %collective-permute-done.10 = bf16[64,1536]{1,0:T(8,128)(2,1)S(1)} collective-permute-done((bf16[64,1536]{1,0:T(8,128)(2,1)}, bf16[64,1536]{1,0:T(8,128)(2,1)S(1)}, u32[]{:S(2)}, u32[]{:S(2)}) %collective-permute-start.10) | collective-permute-done | bytes 196640 | tf_op jit(solution)/shard_map/ppermute | solution.py:12
  54.1 0.2 convolution_add_fusion.7
  54.3 1.9 %collective-permute-done.16 = bf16[64,1536]{1,0:T(8,128)(2,1)S(1)} collective-permute-done((bf16[64,1536]{1,0:T(8,128)(2,1)}, bf16[64,1536]{1,0:T(8,128)(2,1)S(1)}, u32[]{:S(2)}, u32[]{:S(2)}) %collective-permute-start.16) | collective-permute-done | bytes 196640 | tf_op jit(solution)/shard_map/ppermute | solution.py:12
  56.2 0.2 convolution_add_fusion.1
  56.4 1.9 %collective-permute-done.14 = bf16[64,1536]{1,0:T(8,128)(2,1)S(1)} collective-permute-done((bf16[64,1536]{1,0:T(8,128)(2,1)S(1)}, bf16[64,1536]{1,0:T(8,128)(2,1)S(1)}, u32[]{:S(2)}, u32[]{:S(2)}) %collective-permute-start.14) | collective-permute-done | bytes 196640 | tf_op jit(solution)/shard_map/ppermute | solution.py:12
  58.3 0.3 fusion.11
  58.6 1.8 %collective-permute-done.2 = bf16[64,1536]{1,0:T(8,128)(2,1)S(1)} collective-permute-done((bf16[64,1536]{1,0:T(8,128)(2,1)S(1)}, bf16[64,1536]{1,0:T(8,128)(2,1)S(1)}, u32[]{:S(2)}, u32[]{:S(2)}) %collective-permute-start.2) | collective-permute-done | bytes 196640 | tf_op jit(solution)/shard_map/ppermute | solution.py:12
  60.4 0.3 fusion.3
  60.7 1.8 %collective-permute-done.11 = bf16[64,1536]{1,0:T(8,128)(2,1)S(1)} collective-permute-done((bf16[64,1536]{1,0:T(8,128)(2,1)S(1)}, bf16[64,1536]{1,0:T(8,128)(2,1)S(1)}, u32[]{:S(2)}, u32[]{:S(2)}) %collective-permute-start.11) | collective-permute-done | bytes 196640 | tf_op jit(solution)/shard_map/ppermute | solution.py:12
  62.5 0.3 fusion.7
  62.8 1.8 %collective-permute-done.17 = bf16[64,1536]{1,0:T(8,128)(2,1)S(1)} collective-permute-done((bf16[64,1536]{1,0:T(8,128)(2,1)S(1)}, bf16[64,1536]{1,0:T(8,128)(2,1)S(1)}, u32[]{:S(2)}, u32[]{:S(2)}) %collective-permute-start.17) | collective-permute-done | bytes 196640 | tf_op jit(solution)/shard_map/ppermute | solution.py:12
  64.6 0.2 fusion.15
  64.9 0.9 %pad_maximum_fusion = bf16[64,6144]{1,0:T(8,128)(2,1)} fusion(bf16[64,1536]{1,0:T(8,128)(2,1)S(1)} %fusion.15, bf16[64,1536]{1,0:T(8,128)(2,1)S(1)} %fusion.11, bf16[64,1536]{1,0:T(8,128)(2,1)S(1)} %fusion.7, bf16[64,1536]{1,0:T(8,128)(2,1)S(1)} %fusion.3), kind=kLoop, calls=%fused_computation.49 | loop fusion | flops 3145728 | bytes 1572864 | tf_op jit(solution)/shard_map/concatenate | solution.py:77
  (33 shorter events, 0.3 us)
Async XLA Ops:
  0.0 5.7 %copy-start = (bf16[64,6144]{1,0:T(8,128)(2,1)S(1)}, bf16[64,6144]{1,0:T(8,128)(2,1)}, u32[]{:S(2)}) copy-start(bf16[64,6144]{1,0:T(8,128)(2,1)} %param.5) | copy-start | bytes 2359300
  5.1 5.1 %copy-start.3 = (s32[4,32]{1,0:T(4,128)S(1)}, s32[4,32]{1,0:T(4,128)}, u32[]{:S(2)}) copy-start(s32[4,32]{1,0:T(4,128)} %param.9) | copy-start | bytes 1540
  5.1 5.1 %copy-start.1 = (bf16[64,256]{1,0:T(8,128)(2,1)S(1)}, bf16[64,256]{1,0:T(8,128)(2,1)}, u32[]{:S(2)}) copy-start(bf16[64,256]{1,0:T(8,128)(2,1)} %param.6) | copy-start | bytes 98308
  5.2 19.3 %collective-permute-start.3 = (bf16[64,512]{1,0:T(8,128)(2,1)S(1)}, bf16[64,512]{1,0:T(8,128)(2,1)}, u32[]{:S(2)}, u32[]{:S(2)}) collective-permute-start(bf16[64,512]{1,0:T(8,128)(2,1)S(1)} %convolution_convert_fusion), channel_id=1, source_target_pairs={{28,0},{0,4},{4,8},{8,12},{12,16},{16,20},{20,24},{24,28},{29,1},{... | collective-permute-start | bytes 196616 | tf_op jit(solution)/shard_map/ppermute | solution.py:12
  5.7 5.5 %copy-start.2 = (f32[16,16,16]{2,1,0:T(8,128)S(1)}, f32[16,16,16]{2,1,0:T(8,128)}, u32[]{:S(2)}) copy-start(f32[16,16,16]{2,1,0:T(8,128)} %param.8) | copy-start | bytes 49156
  5.7 32.5 %collective-permute-start.12 = (bf16[64,1536]{1,0:T(8,128)(2,1)S(1)}, bf16[64,1536]{1,0:T(8,128)(2,1)}, u32[]{:S(2)}, u32[]{:S(2)}) collective-permute-start(bf16[64,1536]{1,0:T(8,128)(2,1)S(1)} %get-tuple-element.10), channel_id=1, source_target_pairs={{28,0},{0,4},{4,8},{8,12},{12,16},{16,20},{20,24},{24,28},{29,1},{... | collective-permute-start | bytes 589832 | tf_op jit(solution)/shard_map/ppermute | solution.py:12
  8.5 32.4 %collective-permute-start = (bf16[64,1536]{1,0:T(8,128)(2,1)S(1)}, bf16[64,1536]{1,0:T(8,128)(2,1)}, u32[]{:S(2)}, u32[]{:S(2)}) collective-permute-start(bf16[64,1536]{1,0:T(8,128)(2,1)S(1)} %get-tuple-element.7), channel_id=1, source_target_pairs={{28,0},{0,4},{4,8},{8,12},{12,16},{16,20},{20,24},{24,28},{29,1},{... | collective-permute-start | bytes 589832 | tf_op jit(solution)/shard_map/ppermute | solution.py:12
  8.5 34.2 %collective-permute-start.9 = (bf16[64,1536]{1,0:T(8,128)(2,1)S(1)}, bf16[64,1536]{1,0:T(8,128)(2,1)}, u32[]{:S(2)}, u32[]{:S(2)}) collective-permute-start(bf16[64,1536]{1,0:T(8,128)(2,1)S(1)} %get-tuple-element.8), channel_id=1, source_target_pairs={{28,0},{0,4},{4,8},{8,12},{12,16},{16,20},{20,24},{24,28},{29,1},{... | collective-permute-start | bytes 589832 | tf_op jit(solution)/shard_map/ppermute | solution.py:12
  10.2 33.8 %collective-permute-start.15 = (bf16[64,1536]{1,0:T(8,128)(2,1)S(1)}, bf16[64,1536]{1,0:T(8,128)(2,1)}, u32[]{:S(2)}, u32[]{:S(2)}) collective-permute-start(bf16[64,1536]{1,0:T(8,128)(2,1)S(1)} %get-tuple-element.9), channel_id=1, source_target_pairs={{28,0},{0,4},{4,8},{8,12},{12,16},{16,20},{20,24},{24,28},{29,1},{... | collective-permute-start | bytes 589832 | tf_op jit(solution)/shard_map/ppermute | solution.py:12
  24.1 23.6 %slice-start = ((s8[6291456]{0:T(1024)(128)(4,1)}), s8[2097152]{0:T(1024)(128)(4,1)S(1)}, s32[]{:S(2)}) async-start(s8[6291456]{0:T(1024)(128)(4,1)} %bitcast.54), calls=%async_computation | async-start | bytes 4194304
  24.4 5.8 %collective-permute-start.4 = (bf16[64,512]{1,0:T(8,128)(2,1)}, bf16[64,512]{1,0:T(8,128)(2,1)S(1)}, u32[]{:S(2)}, u32[]{:S(2)}) collective-permute-start(bf16[64,512]{1,0:T(8,128)(2,1)} %collective-permute-done.3), channel_id=1, source_target_pairs={{28,0},{0,4},{4,8},{8,12},{12,16},{16,20},{20,24},{24,28},{29,1},{... | collective-permute-start | bytes 196616 | tf_op jit(solution)/shard_map/ppermute | solution.py:12
  30.2 5.5 %collective-permute-start.5 = (bf16[64,512]{1,0:T(8,128)(2,1)S(1)}, bf16[64,512]{1,0:T(8,128)(2,1)S(1)}, u32[]{:S(2)}, u32[]{:S(2)}) collective-permute-start(bf16[64,512]{1,0:T(8,128)(2,1)S(1)} %collective-permute-done.4), channel_id=1, source_target_pairs={{28,0},{0,4},{4,8},{8,12},{12,16},{16,20},{20,24},{24,28},{29,1},{... | collective-permute-start | bytes 196616 | tf_op jit(solution)/shard_map/ppermute | solution.py:12
  35.9 9.3 %collective-permute-start.6 = (f32[64,512]{1,0:T(8,128)S(1)}, f32[64,512]{1,0:T(8,128)S(1)}, u32[]{:S(2)}, u32[]{:S(2)}) collective-permute-start(f32[64,512]{1,0:T(8,128)S(1)} %bitcast.61), channel_id=1, source_target_pairs={{0,1},{1,0},{2,3},{3,2},{4,5},{5,4},{6,7},{7,6},{8,9},{9,8},{10,11... | collective-permute-start | bytes 393224 | tf_op jit(solution)/shard_map/ppermute | solution.py:22
  38.2 9.5 %slice-start.1 = ((s8[6291456]{0:T(1024)(128)(4,1)}), s8[4194304]{0:T(1024)(128)(4,1)S(1)}, s32[]{:S(2)}) async-start(s8[6291456]{0:T(1024)(128)(4,1)} %bitcast.54), calls=%async_computation.1 | async-start | bytes 8388608
  38.2 7.8 %collective-permute-start.8 = (f32[64,512]{1,0:T(8,128)S(1)}, f32[64,512]{1,0:T(8,128)S(1)}, u32[]{:S(2)}, u32[]{:S(2)}) collective-permute-start(f32[64,512]{1,0:T(8,128)S(1)} %bitcast.62), channel_id=1, source_target_pairs={{0,3},{1,2},{2,1},{3,0},{4,7},{5,6},{6,5},{7,4},{8,11},{9,10},{10,... | collective-permute-start | bytes 393224 | tf_op jit(solution)/shard_map/ppermute | solution.py:22
  40.9 6.0 %collective-permute-start.7 = (f32[64,512]{1,0:T(8,128)S(1)}, f32[64,512]{1,0:T(8,128)S(1)}, u32[]{:S(2)}, u32[]{:S(2)}) collective-permute-start(f32[64,512]{1,0:T(8,128)S(1)} %bitcast.63), channel_id=1, source_target_pairs={{0,2},{1,3},{2,0},{3,1},{4,6},{5,7},{6,4},{7,5},{8,10},{9,11},{10,... | collective-permute-start | bytes 393224 | tf_op jit(solution)/shard_map/ppermute | solution.py:22
  42.7 7.2 %collective-permute-start.13 = (bf16[64,1536]{1,0:T(8,128)(2,1)}, bf16[64,1536]{1,0:T(8,128)(2,1)S(1)}, u32[]{:S(2)}, u32[]{:S(2)}) collective-permute-start(bf16[64,1536]{1,0:T(8,128)(2,1)} %collective-permute-done.12), channel_id=1, source_target_pairs={{28,0},{0,4},{4,8},{8,12},{12,16},{16,20},{20,24},{24,28},{29,1},{... | collective-permute-start | bytes 589832 | tf_op jit(solution)/shard_map/ppermute | solution.py:12
  44.0 8.0 %collective-permute-start.1 = (bf16[64,1536]{1,0:T(8,128)(2,1)}, bf16[64,1536]{1,0:T(8,128)(2,1)S(1)}, u32[]{:S(2)}, u32[]{:S(2)}) collective-permute-start(bf16[64,1536]{1,0:T(8,128)(2,1)} %collective-permute-done), channel_id=1, source_target_pairs={{28,0},{0,4},{4,8},{8,12},{12,16},{16,20},{20,24},{24,28},{29,1},{... | collective-permute-start | bytes 589832 | tf_op jit(solution)/shard_map/ppermute | solution.py:12
  45.2 8.9 %collective-permute-start.10 = (bf16[64,1536]{1,0:T(8,128)(2,1)}, bf16[64,1536]{1,0:T(8,128)(2,1)S(1)}, u32[]{:S(2)}, u32[]{:S(2)}) collective-permute-start(bf16[64,1536]{1,0:T(8,128)(2,1)} %collective-permute-done.9), channel_id=1, source_target_pairs={{28,0},{0,4},{4,8},{8,12},{12,16},{16,20},{20,24},{24,28},{29,1},{... | collective-permute-start | bytes 589832 | tf_op jit(solution)/shard_map/ppermute | solution.py:12
  46.1 10.1 %collective-permute-start.16 = (bf16[64,1536]{1,0:T(8,128)(2,1)}, bf16[64,1536]{1,0:T(8,128)(2,1)S(1)}, u32[]{:S(2)}, u32[]{:S(2)}) collective-permute-start(bf16[64,1536]{1,0:T(8,128)(2,1)} %collective-permute-done.15), channel_id=1, source_target_pairs={{28,0},{0,4},{4,8},{8,12},{12,16},{16,20},{20,24},{24,28},{29,1},{... | collective-permute-start | bytes 589832 | tf_op jit(solution)/shard_map/ppermute | solution.py:12
  49.9 8.4 %collective-permute-start.14 = (bf16[64,1536]{1,0:T(8,128)(2,1)S(1)}, bf16[64,1536]{1,0:T(8,128)(2,1)S(1)}, u32[]{:S(2)}, u32[]{:S(2)}) collective-permute-start(bf16[64,1536]{1,0:T(8,128)(2,1)S(1)} %collective-permute-done.13), channel_id=1, source_target_pairs={{28,0},{0,4},{4,8},{8,12},{12,16},{16,20},{20,24},{24,28},{29,1},{... | collective-permute-start | bytes 589832 | tf_op jit(solution)/shard_map/ppermute | solution.py:12
  52.0 8.4 %collective-permute-start.2 = (bf16[64,1536]{1,0:T(8,128)(2,1)S(1)}, bf16[64,1536]{1,0:T(8,128)(2,1)S(1)}, u32[]{:S(2)}, u32[]{:S(2)}) collective-permute-start(bf16[64,1536]{1,0:T(8,128)(2,1)S(1)} %collective-permute-done.1), channel_id=1, source_target_pairs={{28,0},{0,4},{4,8},{8,12},{12,16},{16,20},{20,24},{24,28},{29,1},{... | collective-permute-start | bytes 589832 | tf_op jit(solution)/shard_map/ppermute | solution.py:12
  54.1 8.4 %collective-permute-start.11 = (bf16[64,1536]{1,0:T(8,128)(2,1)S(1)}, bf16[64,1536]{1,0:T(8,128)(2,1)S(1)}, u32[]{:S(2)}, u32[]{:S(2)}) collective-permute-start(bf16[64,1536]{1,0:T(8,128)(2,1)S(1)} %collective-permute-done.10), channel_id=1, source_target_pairs={{28,0},{0,4},{4,8},{8,12},{12,16},{16,20},{20,24},{24,28},{29,1},{... | collective-permute-start | bytes 589832 | tf_op jit(solution)/shard_map/ppermute | solution.py:12
  56.2 8.4 %collective-permute-start.17 = (bf16[64,1536]{1,0:T(8,128)(2,1)S(1)}, bf16[64,1536]{1,0:T(8,128)(2,1)S(1)}, u32[]{:S(2)}, u32[]{:S(2)}) collective-permute-start(bf16[64,1536]{1,0:T(8,128)(2,1)S(1)} %collective-permute-done.16), channel_id=1, source_target_pairs={{28,0},{0,4},{4,8},{8,12},{12,16},{16,20},{20,24},{24,28},{29,1},{... | collective-permute-start | bytes 589832 | tf_op jit(solution)/shard_map/ppermute | solution.py:12
